TPU v7x, 32 devices: a whole 2x2x4 slice. The times are simulated.
32 devices in a mesh: front: 8 (over z, x), col: 4 (over y, core).
Axes of the slice: x: 2, y: 2, z: 4, core: 2. Of those that a mesh axis runs over, the one named last changes fastest.
Arguments:
- leaf_load: bfloat16 [8192, 2048], P('front', 'col'), may hold values from -6 to 6
- leaf_inverse: bfloat16 [8192, 1024], P(('front', 'col')), may hold values from -0.1875 to 0.1875
- leaf_coupling: bfloat16 [4096, 1024], P('front'), may hold values from -0.1875 to 0.1875
- leaf_rowmap: int32 [8, 512], P('front'), may hold values from 0 to 511, each once within a row
- load_first: bfloat16 [2048, 2048], P('front', 'col'), may hold values from -6 to 6
- load_second: bfloat16 [1024, 2048], P('front', 'col'), may hold values from -6 to 6
- load_third: bfloat16 [512, 2048], P('front', 'col'), may hold values from -6 to 6
- inverse_first: bfloat16 [2048, 512], P('front'), may hold values from -0.15625 to 0.15625
- inverse_second: bfloat16 [1024, 512], P('front'), may hold values from -0.15625 to 0.15625
- inverse_third: bfloat16 [512, 512], P('front'), may hold values from -0.15625 to 0.15625
- coupling_first: bfloat16 [512, 2048], P(None, 'front'), may hold values from -0.25 to 0.25
- coupling_second: bfloat16 [512, 1024], P(None, 'front'), may hold values from -0.25 to 0.25
- rowmap_first: int32 [4, 512], replicated, may hold values from 0 to 511, each once within a row
- rowmap_second: int32 [2, 512], replicated, may hold values from 0 to 511, each once within a row
- surface_coupling: bfloat16 [24, 1024, 1024], P('front'), may hold values from -0.125 to 0.125
- neighbor_tiles: int32 [8, 2], replicated, may hold values from 0 to 7, as said below
Outputs:
- volume_solution: bfloat16 [8192, 2048], P('front', 'col')
- surface_tiles: bfloat16 [8192, 2048], P('front', 'col')
- solution_first: bfloat16 [2048, 2048], P('front', 'col')
- solution_second: bfloat16 [1024, 2048], P('front', 'col')
- solution_third: bfloat16 [512, 2048], P('front', 'col')
Inputs may be any that keep to these rules, and one draw needn't show every extreme that they name: Each row of leaf_rowmap is a permutation of the 512 separator rows. Each row of rowmap_first is a permutation of the 512 separator rows. Each row of rowmap_second is a permutation of the 512 separator rows. `neighbor_tiles`: row f names two different tiles, neither equal to f, each within 2 of f; counting each front's own tile, every tile receives 1 to 5 contributions, and some tile receives 5.
All inputs are finite; a program needn't handle non-finite values.
Results may differ from a plain program's by a relative error of at most 0.015.
Values may be sent and summed in bfloat16 or wider, within the bound.
A program may use at most 128 MiB of HBM per device.

v0:
```python
import jax
import jax.numpy as jnp
from jax import lax
from jax.sharding import PartitionSpec as P


def from_partner(x, axis, bit):
    return lax.ppermute(x, axis, [(i, i ^ 1 << bit) for i in range(lax.axis_size(axis))])


def from_behind(value, axis, steps):
    count = lax.axis_size(axis)
    leading, last = (max(0, -steps), min(count, count - steps))
    return lax.ppermute(value, axis, [(source, source + steps) for source in range(leading, last)])


def climb_tree(own_term, bit_count):
    position = lax.axis_index("front")
    current = own_term
    for level_bit in range(bit_count):
        half_rows = current.shape[0] // 2
        is_upper = position >> level_bit & 1 == 1
        kept_part = jnp.where(is_upper, current[half_rows:], current[:half_rows])
        given_part = jnp.where(is_upper, current[:half_rows], current[half_rows:])
        current = kept_part + from_partner(given_part, "front", level_bit)
    for level_bit in reversed(range(bit_count)):
        partner = from_partner(current.astype(jnp.bfloat16), "front", level_bit).astype(
            current.dtype
        )
        is_upper = position >> level_bit & 1 == 1
        current = jnp.where(
            is_upper,
            jnp.concatenate([partner, current], axis=0),
            jnp.concatenate([current, partner], axis=0),
        )
    return current


def spread(row_block, bit_count):
    position = lax.axis_index("front")
    for level_bit in range(bit_count):
        partner = from_partner(row_block, "front", level_bit)
        is_upper = position >> level_bit & 1 == 1
        row_block = jnp.where(
            is_upper,
            jnp.concatenate([partner, row_block], axis=0),
            jnp.concatenate([row_block, partner], axis=0),
        )
    return row_block


def pull_back(coupling, lifted):
    return lax.dot_general(
        coupling, lifted, (((0,), (0,)), ((), ())), preferred_element_type=jnp.float32
    )


def local(
    leaf_load,
    leaf_inverse,
    leaf_coupling,
    leaf_rowmap,
    load_first,
    load_second,
    load_third,
    inverse_first,
    inverse_second,
    inverse_third,
    coupling_first,
    coupling_second,
    rowmap_first,
    rowmap_second,
    surface_coupling,
    neighbor_tiles,
):
    position = lax.axis_index("front")
    front_count = lax.axis_size("front")
    factor = lax.all_gather(leaf_inverse, "col", axis=0, tiled=True)
    first_solve = jnp.dot(factor, leaf_load, preferred_element_type=jnp.float32).astype(
        jnp.bfloat16
    )
    sep_order = leaf_coupling.shape[0]
    panel_cols = leaf_load.shape[1]
    partial_value = jnp.dot(leaf_coupling, first_solve, preferred_element_type=jnp.float32)[
        leaf_rowmap[0]
    ]
    load_list = (load_first, load_second, load_third)
    inverses = (inverse_first, inverse_second, inverse_third)
    couplings = (coupling_first, coupling_second)
    rowmaps = (rowmap_first, rowmap_second)
    solved = []
    for level_index in range(3):
        row_count = load_list[level_index].shape[0]
        offset = position % 2 ** (level_index + 1) * row_count
        embedded = lax.dynamic_update_slice_in_dim(
            jnp.zeros((sep_order, panel_cols), jnp.float32),
            load_list[level_index].astype(jnp.float32),
            offset,
            0,
        )
        right_side = climb_tree(embedded - partial_value, level_index + 1).astype(jnp.bfloat16)
        solution = jnp.dot(
            inverses[level_index], right_side, preferred_element_type=jnp.float32
        ).astype(jnp.bfloat16)
        solved.append(solution)
        if level_index < 2:
            row_map = lax.dynamic_index_in_dim(
                rowmaps[level_index], position >> level_index + 1, 0, keepdims=False
            )
            partial_value = jnp.dot(
                couplings[level_index], solution, preferred_element_type=jnp.float32
            )[row_map]
    parent_rows = solved[2]
    results = [None, None, parent_rows]
    for level_index in (1, 0):
        full_vector = spread(parent_rows, level_index + 2)
        row_map = lax.dynamic_index_in_dim(
            rowmaps[level_index], position >> level_index + 1, 0, keepdims=False
        )
        lifted = jnp.zeros((sep_order, panel_cols), jnp.bfloat16).at[row_map].set(full_vector)
        pieces = pull_back(couplings[level_index], lifted).astype(jnp.bfloat16)
        full_pull = spread(pieces, level_index + 1)
        parent_rows = (
            solved[level_index].astype(jnp.float32)
            - jnp.dot(inverses[level_index], full_pull, preferred_element_type=jnp.float32)
        ).astype(jnp.bfloat16)
        results[level_index] = parent_rows
    full_vector = spread(parent_rows, 1)
    lifted = jnp.zeros((sep_order, panel_cols), jnp.bfloat16).at[leaf_rowmap[0]].set(full_vector)
    pulled = pull_back(leaf_coupling, lifted).astype(jnp.bfloat16)
    volume = (
        first_solve.astype(jnp.float32)
        - jnp.dot(factor, pulled, preferred_element_type=jnp.float32)
    ).astype(jnp.bfloat16)
    contribution = jnp.einsum(
        "stf,fp->stp", surface_coupling, volume, preferred_element_type=jnp.float32
    ).astype(jnp.bfloat16)
    tile_sums = contribution[0].astype(jnp.float32)
    for source in (-2, -1, 1, 2):
        arrived = from_behind(contribution[1:], "front", -source)
        anchor = jnp.clip(position + source, 0, front_count - 1)
        aimed_tiles = lax.dynamic_index_in_dim(neighbor_tiles, anchor, 0, keepdims=False)
        matches = (aimed_tiles == position)[:, None, None]
        tile_sums = tile_sums + jnp.sum(
            jnp.where(matches, arrived.astype(jnp.float32), 0.0), axis=0
        )
    return (volume, tile_sums.astype(jnp.bfloat16), results[0], results[1], results[2])


def solution(mesh):
    return jax.shard_map(
        local,
        mesh=mesh,
        in_specs=(
            P("front", "col"),
            P(("front", "col"), None),
            P("front", None),
            P("front", None),
            P("front", "col"),
            P("front", "col"),
            P("front", "col"),
            P("front", None),
            P("front", None),
            P("front", None),
            P(None, "front"),
            P(None, "front"),
            P(),
            P(),
            P("front", None, None),
            P(),
        ),
        out_specs=(
            P("front", "col"),
            P("front", "col"),
            P("front", "col"),
            P("front", "col"),
            P("front", "col"),
        ),
        check_vma=False,
    )
```

profile of v0, /device:TPU:0, one launch (start us, length us, event | category | flops | bytes accessed | tf_op | source)
XLA Modules:
  0.0 318.5 jit_solution(6423248784681602663)
XLA Ops:
  9.7 1.8 convert_dynamic-update-slice_fusion
  11.5 23.4 %all-gather.2.cloned.1.call-done = bf16[1024,1024]{1,0:T(8,128)(2,1)} async-done(((bf16[256,1024]{1,0:T(8,128)(2,1)}), bf16[1024,1024]{1,0:T(8,128)(2,1)}) %all-gather.2.cloned.1.call-update) | async-done | bytes 2097168 | tf_op jit(solution)/shard_map/all_gather | solution.py:78
  34.9 2.8 convolution_convert_fusion
  39.8 1.6 gather_fusion
  41.5 1.4 sub.20
  43.0 1.5 collective-permute-start
  45.3 11.9 %collective-permute-done = f32[256,512]{1,0:T(8,128)S(1)} collective-permute-done((f32[256,512]{1,0:T(8,128)S(1)}, f32[256,512]{1,0:T(8,128)S(1)}, u32[]{:S(2)}, u32[]{:S(2)}) %collective-permute-start) | collective-permute-done | bytes 524320 | tf_op jit(solution)/shard_map/ppermute | solution.py:8
  57.3 1.5 collective-permute-start.1
  60.7 4.3 %collective-permute-done.1 = bf16[256,512]{1,0:T(8,128)(2,1)S(1)} collective-permute-done((bf16[256,512]{1,0:T(8,128)(2,1)S(1)}, bf16[256,512]{1,0:T(8,128)(2,1)S(1)}, u32[]{:S(2)}, u32[]{:S(2)}) %collective-permute-start.1) | collective-permute-done | bytes 262176 | tf_op jit(solution)/shard_map/ppermute | solution.py:8
  67.7 1.6 gather_fusion.1
  70.9 1.5 collective-permute-start.2
  72.4 10.8 %collective-permute-done.2 = f32[256,512]{1,0:T(8,128)S(1)} collective-permute-done((f32[256,512]{1,0:T(8,128)S(1)}, f32[256,512]{1,0:T(8,128)S(1)}, u32[]{:S(2)}, u32[]{:S(2)}) %collective-permute-start.2) | collective-permute-done | bytes 524320 | tf_op jit(solution)/shard_map/ppermute | solution.py:8
  83.5 1.5 collective-permute-start.3
  85.0 5.7 %collective-permute-done.3 = f32[128,512]{1,0:T(8,128)S(1)} collective-permute-done((f32[128,512]{1,0:T(8,128)S(1)}, f32[128,512]{1,0:T(8,128)S(1)}, u32[]{:S(2)}, u32[]{:S(2)}) %collective-permute-start.3) | collective-permute-done | bytes 262176 | tf_op jit(solution)/shard_map/ppermute | solution.py:8
  90.8 1.5 collective-permute-start.4
  92.3 3.5 %collective-permute-done.4 = bf16[128,512]{1,0:T(8,128)(2,1)S(1)} collective-permute-done((bf16[128,512]{1,0:T(8,128)(2,1)S(1)}, bf16[128,512]{1,0:T(8,128)(2,1)S(1)}, u32[]{:S(2)}, u32[]{:S(2)}) %collective-permute-start.4) | collective-permute-done | bytes 131104 | tf_op jit(solution)/shard_map/ppermute | solution.py:8
  95.9 1.5 collective-permute-start.5
  97.6 4.7 %collective-permute-done.5 = bf16[256,512]{1,0:T(8,128)(2,1)S(1)} collective-permute-done((bf16[256,512]{1,0:T(8,128)(2,1)S(1)}, bf16[256,512]{1,0:T(8,128)(2,1)S(1)}, u32[]{:S(2)}, u32[]{:S(2)}) %collective-permute-start.5) | collective-permute-done | bytes 262176 | tf_op jit(solution)/shard_map/ppermute | solution.py:8
  103.9 1.6 gather_fusion.2
  107.1 1.5 collective-permute-start.6
  108.6 7.7 %collective-permute-done.6 = f32[256,512]{1,0:T(8,128)S(1)} collective-permute-done((f32[256,512]{1,0:T(8,128)S(1)}, f32[256,512]{1,0:T(8,128)S(1)}, u32[]{:S(2)}, u32[]{:S(2)}) %collective-permute-start.6) | collective-permute-done | bytes 524320 | tf_op jit(solution)/shard_map/ppermute | solution.py:8
  116.5 1.5 collective-permute-start.7
  118.1 5.3 %collective-permute-done.7 = f32[128,512]{1,0:T(8,128)S(1)} collective-permute-done((f32[128,512]{1,0:T(8,128)S(1)}, f32[128,512]{1,0:T(8,128)S(1)}, u32[]{:S(2)}, u32[]{:S(2)}) %collective-permute-start.7) | collective-permute-done | bytes 262176 | tf_op jit(solution)/shard_map/ppermute | solution.py:8
  123.5 2.4 collective-permute-start.8
  125.8 4.2 %collective-permute-done.8 = f32[64,512]{1,0:T(8,128)S(1)} collective-permute-done((f32[64,512]{1,0:T(8,128)S(1)}, f32[64,512]{1,0:T(8,128)S(1)}, u32[]{:S(2)}, u32[]{:S(2)}) %collective-permute-start.8) | collective-permute-done | bytes 131104 | tf_op jit(solution)/shard_map/ppermute | solution.py:8
  130.1 2.9 collective-permute-start.9
  133.0 2.3 collective-permute-done.9
  135.3 2.1 collective-permute-start.10
  137.5 2.9 collective-permute-done.10
  140.5 1.5 collective-permute-start.11
  142.0 4.9 %collective-permute-done.11 = bf16[256,512]{1,0:T(8,128)(2,1)S(1)} collective-permute-done((bf16[256,512]{1,0:T(8,128)(2,1)S(1)}, bf16[256,512]{1,0:T(8,128)(2,1)S(1)}, u32[]{:S(2)}, u32[]{:S(2)}) %collective-permute-start.11) | collective-permute-done | bytes 262176 | tf_op jit(solution)/shard_map/ppermute | solution.py:8
  147.2 1.5 collective-permute-start.12
  148.8 2.8 collective-permute-done.12
  151.6 2.1 collective-permute-start.13
  153.7 2.9 collective-permute-done.13
  156.7 3.0 collective-permute-start.14
  159.7 6.7 %collective-permute-done.14 = bf16[256,512]{1,0:T(8,128)(2,1)S(1)} collective-permute-done((bf16[256,512]{1,0:T(8,128)(2,1)S(1)}, bf16[256,512]{1,0:T(8,128)(2,1)S(1)}, u32[]{:S(2)}, u32[]{:S(2)}) %collective-permute-start.14) | collective-permute-done | bytes 262176 | tf_op jit(solution)/shard_map/ppermute | solution.py:8
  166.4 2.8 scatter_custom_fusion
  169.5 1.5 collective-permute-start.15
  171.0 3.5 %collective-permute-done.15 = bf16[128,512]{1,0:T(8,128)(2,1)S(1)} collective-permute-done((bf16[128,512]{1,0:T(8,128)(2,1)S(1)}, bf16[128,512]{1,0:T(8,128)(2,1)S(1)}, u32[]{:S(2)}, u32[]{:S(2)}) %collective-permute-start.15) | collective-permute-done | bytes 131104 | tf_op jit(solution)/shard_map/ppermute | solution.py:8
  174.6 1.9 collective-permute-start.16
  176.5 4.6 %collective-permute-done.16 = bf16[256,512]{1,0:T(8,128)(2,1)S(1)} collective-permute-done((bf16[256,512]{1,0:T(8,128)(2,1)S(1)}, bf16[256,512]{1,0:T(8,128)(2,1)S(1)}, u32[]{:S(2)}, u32[]{:S(2)}) %collective-permute-start.16) | collective-permute-done | bytes 262176 | tf_op jit(solution)/shard_map/ppermute | solution.py:8
  181.4 1.5 collective-permute-start.17
  182.9 3.5 %collective-permute-done.17 = bf16[128,512]{1,0:T(8,128)(2,1)S(1)} collective-permute-done((bf16[128,512]{1,0:T(8,128)(2,1)S(1)}, bf16[128,512]{1,0:T(8,128)(2,1)S(1)}, u32[]{:S(2)}, u32[]{:S(2)}) %collective-permute-start.17) | collective-permute-done | bytes 131104 | tf_op jit(solution)/shard_map/ppermute | solution.py:8
  186.5 1.9 collective-permute-start.18
  188.3 4.6 %collective-permute-done.18 = bf16[256,512]{1,0:T(8,128)(2,1)S(1)} collective-permute-done((bf16[256,512]{1,0:T(8,128)(2,1)S(1)}, bf16[256,512]{1,0:T(8,128)(2,1)S(1)}, u32[]{:S(2)}, u32[]{:S(2)}) %collective-permute-start.18) | collective-permute-done | bytes 262176 | tf_op jit(solution)/shard_map/ppermute | solution.py:8
  192.9 2.6 scatter_custom_fusion.1
  195.9 1.5 collective-permute-start.19
  197.4 4.9 %collective-permute-done.19 = bf16[256,512]{1,0:T(8,128)(2,1)S(1)} collective-permute-done((bf16[256,512]{1,0:T(8,128)(2,1)S(1)}, bf16[256,512]{1,0:T(8,128)(2,1)S(1)}, u32[]{:S(2)}, u32[]{:S(2)}) %collective-permute-start.19) | collective-permute-done | bytes 262176 | tf_op jit(solution)/shard_map/ppermute | solution.py:8
  202.7 1.5 collective-permute-start.20
  204.2 4.9 %collective-permute-done.20 = bf16[256,512]{1,0:T(8,128)(2,1)S(1)} collective-permute-done((bf16[256,512]{1,0:T(8,128)(2,1)S(1)}, bf16[256,512]{1,0:T(8,128)(2,1)S(1)}, u32[]{:S(2)}, u32[]{:S(2)}) %collective-permute-start.20) | collective-permute-done | bytes 262176 | tf_op jit(solution)/shard_map/ppermute | solution.py:8
  209.1 2.6 scatter_custom_fusion.2
  211.8 3.7 %fusion.4 = bf16[1024,512]{1,0:T(8,128)(2,1)S(1)} fusion(bf16[1024,512]{1,0:T(8,128)(2,1)} %copy-done.22, bf16[1024,1024]{1,0:T(8,128)(2,1)} %all-gather.2.cloned.1.call-done, bf16[512,512]{1,0:T(8,128)(2,1)S(1)} %scatter_custom_fusion.2, bf16[512,1024]{1,0:T(8,128)(2,1)S(1)} %copy-done), kind=kOutput, calls=%fused_computation.17 | convolution fusion | flops 1612709888 | bytes 5767168 | tf_op jit(solution)/shard_map/dot_general | solution.py:133
  216.4 6.6 %convert_bitcast_fusion = bf16[3,1024,512]{1,2,0:T(8,128)(2,1)S(1)} fusion(bf16[3,1024,1024]{2,1,0:T(8,128)(2,1)} %param.30, bf16[1024,512]{1,0:T(8,128)(2,1)S(1)} %fusion.4), kind=kOutput, calls=%fused_computation.10 | convolution fusion | flops 3222798336 | bytes 10485760 | tf_op jit(solution)/shard_map/stf,fp->stp/dot_general | solution.py:135
  223.2 1.4 copy-done.2
  227.2 6.0 %collective-permute-start.22 = (bf16[2,1024,512]{1,2,0:T(8,128)(2,1)S(1)}, bf16[2,1024,512]{1,2,0:T(8,128)(2,1)}, u32[]{:S(2)}, u32[]{:S(2)}) collective-permute-start(bf16[2,1024,512]{1,2,0:T(8,128)(2,1)S(1)} %slice.90), channel_id=1, source_target_pairs={{0,4},{4,8},{8,12},{12,16},{16,20},{20,24},{24,28},{1,5},{5,9},{9,... | collective-permute-start | bytes 6291464 | tf_op jit(solution)/shard_map/ppermute | solution.py:14
  233.2 4.5 %collective-permute-start.21 = (bf16[2,1024,512]{1,2,0:T(8,128)(2,1)S(1)}, bf16[2,1024,512]{1,2,0:T(8,128)(2,1)}, u32[]{:S(2)}, u32[]{:S(2)}) collective-permute-start(bf16[2,1024,512]{1,2,0:T(8,128)(2,1)S(1)} %slice.90), channel_id=1, source_target_pairs={{0,8},{4,12},{8,16},{12,20},{16,24},{20,28},{1,9},{5,13},{9,17},{1... | collective-permute-start | bytes 6291464 | tf_op jit(solution)/shard_map/ppermute | solution.py:14
  237.9 37.3 %collective-permute-done.24 = bf16[2,1024,512]{1,2,0:T(8,128)(2,1)} collective-permute-done((bf16[2,1024,512]{1,2,0:T(8,128)(2,1)S(1)}, bf16[2,1024,512]{1,2,0:T(8,128)(2,1)}, u32[]{:S(2)}, u32[]{:S(2)}) %collective-permute-start.24) | collective-permute-done | bytes 2097184 | tf_op jit(solution)/shard_map/ppermute | solution.py:14
  275.2 2.6 select_reduce_fusion
  277.8 2.6 select_reduce_fusion.1
  280.4 22.5 %collective-permute-done.22 = bf16[2,1024,512]{1,2,0:T(8,128)(2,1)} collective-permute-done((bf16[2,1024,512]{1,2,0:T(8,128)(2,1)S(1)}, bf16[2,1024,512]{1,2,0:T(8,128)(2,1)}, u32[]{:S(2)}, u32[]{:S(2)}) %collective-permute-start.22) | collective-permute-done | bytes 2097184 | tf_op jit(solution)/shard_map/ppermute | solution.py:14
  302.9 2.6 select_reduce_fusion.2
  305.4 2.6 select_reduce_fusion.3
  308.0 2.3 fusion.3
  (98 shorter events, 22.5 us)
Async XLA Ops:
  7.2 31.6 %copy-start = (bf16[512,1024]{1,0:T(8,128)(2,1)S(1)}, bf16[512,1024]{1,0:T(8,128)(2,1)}, u32[]{:S(2)}) copy-start(bf16[512,1024]{1,0:T(8,128)(2,1)} %param.18) | copy-start | bytes 3145732
  7.2 27.7 %copy-start.16 = (bf16[1024,512]{1,0:T(8,128)(2,1)S(1)}, bf16[1024,512]{1,0:T(8,128)(2,1)}, u32[]{:S(2)}) copy-start(bf16[1024,512]{1,0:T(8,128)(2,1)} %param.16) | copy-start | bytes 3145732
  7.2 27.7 %all-gather.2.cloned.1.call-start = ((), (), s32[]{:S(2)}) async-start(), calls=%async_computation | async-start | bytes 2621440 | tf_op jit(solution)/shard_map/all_gather | solution.py:78
  37.8 1.0 copy-start.22
  41.5 3.1 copy-start.15
  42.9 17.1 %copy-start.11 = (bf16[128,512]{1,0:T(8,128)(2,1)S(1)}, bf16[128,512]{1,0:T(8,128)(2,1)}, u32[]{:S(2)}) copy-start(bf16[128,512]{1,0:T(8,128)(2,1)} %param.21) | copy-start | bytes 393220
  43.0 14.1 %collective-permute-start = (f32[256,512]{1,0:T(8,128)S(1)}, f32[256,512]{1,0:T(8,128)S(1)}, u32[]{:S(2)}, u32[]{:S(2)}) collective-permute-start(f32[256,512]{1,0:T(8,128)S(1)} %slice_select_fusion.2), channel_id=1, source_target_pairs={{0,4},{4,0},{8,12},{12,8},{16,20},{20,16},{24,28},{28,24},{1,5},{5... | collective-permute-start | bytes 1572872 | tf_op jit(solution)/shard_map/ppermute | solution.py:8
  57.3 9.7 %copy-start.3 = (bf16[512,256]{1,0:T(8,128)(2,1)S(1)}, bf16[512,256]{1,0:T(8,128)(2,1)}, u32[]{:S(2)}) copy-start(bf16[512,256]{1,0:T(8,128)(2,1)} %param.26) | copy-start | bytes 786436
  57.3 7.7 %collective-permute-start.1 = (bf16[256,512]{1,0:T(8,128)(2,1)S(1)}, bf16[256,512]{1,0:T(8,128)(2,1)S(1)}, u32[]{:S(2)}, u32[]{:S(2)}) collective-permute-start(bf16[256,512]{1,0:T(8,128)(2,1)S(1)} %select_add_fusion.2), channel_id=1, source_target_pairs={{0,4},{4,0},{8,12},{12,8},{16,20},{20,16},{24,28},{28,24},{1,5},{5... | collective-permute-start | bytes 786440 | tf_op jit(solution)/shard_map/ppermute | solution.py:8
  66.3 0.7 copy-start.6
  70.9 12.4 %collective-permute-start.2 = (f32[256,512]{1,0:T(8,128)S(1)}, f32[256,512]{1,0:T(8,128)S(1)}, u32[]{:S(2)}, u32[]{:S(2)}) collective-permute-start(f32[256,512]{1,0:T(8,128)S(1)} %slice_select_fusion.1), channel_id=1, source_target_pairs={{0,4},{4,0},{8,12},{12,8},{16,20},{20,16},{24,28},{28,24},{1,5},{5... | collective-permute-start | bytes 1572872 | tf_op jit(solution)/shard_map/ppermute | solution.py:8
  83.4 14.1 %copy-start.12 = (bf16[64,512]{1,0:T(8,128)(2,1)S(1)}, bf16[64,512]{1,0:T(8,128)(2,1)}, u32[]{:S(2)}) copy-start(bf16[64,512]{1,0:T(8,128)(2,1)} %param.22) | copy-start | bytes 196612
  83.4 18.9 %copy-start.18 = (bf16[128,512]{1,0:T(8,128)(2,1)S(1)}, bf16[128,512]{1,0:T(8,128)(2,1)}, u32[]{:S(2)}) copy-start(bf16[128,512]{1,0:T(8,128)(2,1)} %param.24) | copy-start | bytes 393220
  83.5 7.2 %collective-permute-start.3 = (f32[128,512]{1,0:T(8,128)S(1)}, f32[128,512]{1,0:T(8,128)S(1)}, u32[]{:S(2)}, u32[]{:S(2)}) collective-permute-start(f32[128,512]{1,0:T(8,128)S(1)} %slice_select_fusion.4), channel_id=1, source_target_pairs={{0,8},{4,12},{8,0},{12,4},{16,24},{20,28},{24,16},{28,20},{1,9},{5... | collective-permute-start | bytes 786440 | tf_op jit(solution)/shard_map/ppermute | solution.py:8
  90.7 12.5 %copy-start.4 = (bf16[512,128]{1,0:T(8,128)(2,1)S(1)}, bf16[512,128]{1,0:T(8,128)(2,1)}, u32[]{:S(2)}) copy-start(bf16[512,128]{1,0:T(8,128)(2,1)} %param.27) | copy-start | bytes 393220
  90.8 5.0 %collective-permute-start.4 = (bf16[128,512]{1,0:T(8,128)(2,1)S(1)}, bf16[128,512]{1,0:T(8,128)(2,1)S(1)}, u32[]{:S(2)}, u32[]{:S(2)}) collective-permute-start(bf16[128,512]{1,0:T(8,128)(2,1)S(1)} %select_add_fusion.4), channel_id=1, source_target_pairs={{0,8},{4,12},{8,0},{12,4},{16,24},{20,28},{24,16},{28,20},{1,9},{5... | collective-permute-start | bytes 393224 | tf_op jit(solution)/shard_map/ppermute | solution.py:8
  95.9 6.4 %collective-permute-start.5 = (bf16[256,512]{1,0:T(8,128)(2,1)S(1)}, bf16[256,512]{1,0:T(8,128)(2,1)S(1)}, u32[]{:S(2)}, u32[]{:S(2)}) collective-permute-start(bf16[256,512]{1,0:T(8,128)(2,1)S(1)} %maximum_select_fusion.3), channel_id=1, source_target_pairs={{0,4},{4,0},{8,12},{12,8},{16,20},{20,16},{24,28},{28,24},{1,5},{5... | collective-permute-start | bytes 786440 | tf_op jit(solution)/shard_map/ppermute | solution.py:8
  97.6 5.0 %copy-start.1 = (f32[512,512]{1,0:T(8,128)}, f32[512,512]{1,0:T(8,128)S(1)}, u32[]{:S(2)}) copy-start(f32[512,512]{1,0:T(8,128)S(1)} %convert_dynamic-update-slice_fusion.2) | copy-start | bytes 3145732
  102.6 0.7 copy-start.9
  107.1 9.2 %collective-permute-start.6 = (f32[256,512]{1,0:T(8,128)S(1)}, f32[256,512]{1,0:T(8,128)S(1)}, u32[]{:S(2)}, u32[]{:S(2)}) collective-permute-start(f32[256,512]{1,0:T(8,128)S(1)} %slice_select_fusion), channel_id=1, source_target_pairs={{0,4},{4,0},{8,12},{12,8},{16,20},{20,16},{24,28},{28,24},{1,5},{5... | collective-permute-start | bytes 1572872 | tf_op jit(solution)/shard_map/ppermute | solution.py:8
  116.5 30.5 %copy-start.20 = (bf16[64,512]{1,0:T(8,128)(2,1)S(1)}, bf16[64,512]{1,0:T(8,128)(2,1)}, u32[]{:S(2)}) copy-start(bf16[64,512]{1,0:T(8,128)(2,1)} %param.25) | copy-start | bytes 196612
  116.5 6.9 %collective-permute-start.7 = (f32[128,512]{1,0:T(8,128)S(1)}, f32[128,512]{1,0:T(8,128)S(1)}, u32[]{:S(2)}, u32[]{:S(2)}) collective-permute-start(f32[128,512]{1,0:T(8,128)S(1)} %slice_select_fusion.3), channel_id=1, source_target_pairs={{0,8},{4,12},{8,0},{12,4},{16,24},{20,28},{24,16},{28,20},{1,9},{5... | collective-permute-start | bytes 786440 | tf_op jit(solution)/shard_map/ppermute | solution.py:8
  123.5 6.6 %collective-permute-start.8 = (f32[64,512]{1,0:T(8,128)S(1)}, f32[64,512]{1,0:T(8,128)S(1)}, u32[]{:S(2)}, u32[]{:S(2)}) collective-permute-start(f32[64,512]{1,0:T(8,128)S(1)} %slice_select_fusion.5), channel_id=1, source_target_pairs={{0,16},{4,20},{8,24},{12,28},{16,0},{20,4},{24,8},{28,12},{1,17},{... | collective-permute-start | bytes 393224 | tf_op jit(solution)/shard_map/ppermute | solution.py:8
  130.1 5.2 %collective-permute-start.9 = (bf16[64,512]{1,0:T(8,128)(2,1)S(1)}, bf16[64,512]{1,0:T(8,128)(2,1)S(1)}, u32[]{:S(2)}, u32[]{:S(2)}) collective-permute-start(bf16[64,512]{1,0:T(8,128)(2,1)S(1)} %select_add_fusion.5), channel_id=1, source_target_pairs={{0,16},{4,20},{8,24},{12,28},{16,0},{20,4},{24,8},{28,12},{1,17},{... | collective-permute-start | bytes 196616 | tf_op jit(solution)/shard_map/ppermute | solution.py:8
  135.3 5.1 %collective-permute-start.10 = (bf16[128,512]{1,0:T(8,128)(2,1)S(1)}, bf16[128,512]{1,0:T(8,128)(2,1)S(1)}, u32[]{:S(2)}, u32[]{:S(2)}) collective-permute-start(bf16[128,512]{1,0:T(8,128)(2,1)S(1)} %maximum_select_fusion.15), channel_id=1, source_target_pairs={{0,8},{4,12},{8,0},{12,4},{16,24},{20,28},{24,16},{28,20},{1,9},{5... | collective-permute-start | bytes 393224 | tf_op jit(solution)/shard_map/ppermute | solution.py:8
  140.5 6.4 %collective-permute-start.11 = (bf16[256,512]{1,0:T(8,128)(2,1)S(1)}, bf16[256,512]{1,0:T(8,128)(2,1)S(1)}, u32[]{:S(2)}, u32[]{:S(2)}) collective-permute-start(bf16[256,512]{1,0:T(8,128)(2,1)S(1)} %maximum_select_fusion.4), channel_id=1, source_target_pairs={{0,4},{4,0},{8,12},{12,8},{16,20},{20,16},{24,28},{28,24},{1,5},{5... | collective-permute-start | bytes 786440 | tf_op jit(solution)/shard_map/ppermute | solution.py:8
  147.2 12.5 %copy-start.13 = (bf16[64,512]{1,0:T(8,128)(2,1)}, bf16[64,512]{1,0:T(8,128)(2,1)S(1)}, u32[]{:S(2)}) copy-start(bf16[64,512]{1,0:T(8,128)(2,1)S(1)} %fusion.11) | copy-start | bytes 196612
  147.2 33.8 %copy-start.10 = (bf16[512,128]{0,1:T(8,128)(2,1)S(1)}, bf16[512,128]{0,1:T(8,128)(2,1)}, u32[]{:S(2)}) copy-start(bf16[512,128]{0,1:T(8,128)(2,1)} %copy-done.9) | copy-start | bytes 393220
  147.2 33.8 %copy-start.19 = (bf16[128,512]{1,0:T(8,128)(2,1)S(1)}, bf16[128,512]{1,0:T(8,128)(2,1)}, u32[]{:S(2)}) copy-start(bf16[128,512]{1,0:T(8,128)(2,1)} %param.24) | copy-start | bytes 393220
  147.2 4.3 %collective-permute-start.12 = (bf16[64,512]{1,0:T(8,128)(2,1)S(1)}, bf16[64,512]{1,0:T(8,128)(2,1)S(1)}, u32[]{:S(2)}, u32[]{:S(2)}) collective-permute-start(bf16[64,512]{1,0:T(8,128)(2,1)S(1)} %fusion.11), channel_id=1, source_target_pairs={{0,4},{4,0},{8,12},{12,8},{16,20},{20,16},{24,28},{28,24},{1,5},{5... | collective-permute-start | bytes 196616 | tf_op jit(solution)/shard_map/ppermute | solution.py:8
  151.6 5.0 %collective-permute-start.13 = (bf16[128,512]{1,0:T(8,128)(2,1)S(1)}, bf16[128,512]{1,0:T(8,128)(2,1)S(1)}, u32[]{:S(2)}, u32[]{:S(2)}) collective-permute-start(bf16[128,512]{1,0:T(8,128)(2,1)S(1)} %maximum_select_fusion.19), channel_id=1, source_target_pairs={{0,8},{4,12},{8,0},{12,4},{16,24},{20,28},{24,16},{28,20},{1,9},{5... | collective-permute-start | bytes 393224 | tf_op jit(solution)/shard_map/ppermute | solution.py:8
  156.7 9.7 %collective-permute-start.14 = (bf16[256,512]{1,0:T(8,128)(2,1)S(1)}, bf16[256,512]{1,0:T(8,128)(2,1)S(1)}, u32[]{:S(2)}, u32[]{:S(2)}) collective-permute-start(bf16[256,512]{1,0:T(8,128)(2,1)S(1)} %maximum_select_fusion.16), channel_id=1, source_target_pairs={{0,16},{4,20},{8,24},{12,28},{16,0},{20,4},{24,8},{28,12},{1,17},{... | collective-permute-start | bytes 786440 | tf_op jit(solution)/shard_map/ppermute | solution.py:8
  169.5 5.0 %collective-permute-start.15 = (bf16[128,512]{1,0:T(8,128)(2,1)S(1)}, bf16[128,512]{1,0:T(8,128)(2,1)S(1)}, u32[]{:S(2)}, u32[]{:S(2)}) collective-permute-start(bf16[128,512]{1,0:T(8,128)(2,1)S(1)} %fusion.9), channel_id=1, source_target_pairs={{0,4},{4,0},{8,12},{12,8},{16,20},{20,16},{24,28},{28,24},{1,5},{5... | collective-permute-start | bytes 393224 | tf_op jit(solution)/shard_map/ppermute | solution.py:8
  174.6 27.7 %copy-start.7 = (bf16[512,256]{0,1:T(8,128)(2,1)S(1)}, bf16[512,256]{0,1:T(8,128)(2,1)}, u32[]{:S(2)}) copy-start(bf16[512,256]{0,1:T(8,128)(2,1)} %copy-done.6) | copy-start | bytes 786436
  174.6 27.7 %copy-start.17 = (bf16[256,512]{1,0:T(8,128)(2,1)S(1)}, bf16[256,512]{1,0:T(8,128)(2,1)}, u32[]{:S(2)}) copy-start(bf16[256,512]{1,0:T(8,128)(2,1)} %param.23) | copy-start | bytes 786436
  174.6 6.4 %collective-permute-start.16 = (bf16[256,512]{1,0:T(8,128)(2,1)S(1)}, bf16[256,512]{1,0:T(8,128)(2,1)S(1)}, u32[]{:S(2)}, u32[]{:S(2)}) collective-permute-start(bf16[256,512]{1,0:T(8,128)(2,1)S(1)} %maximum_select_fusion.17), channel_id=1, source_target_pairs={{0,8},{4,12},{8,0},{12,4},{16,24},{20,28},{24,16},{28,20},{1,9},{5... | collective-permute-start | bytes 786440 | tf_op jit(solution)/shard_map/ppermute | solution.py:8
  181.4 21.3 %copy-start.8 = (bf16[128,512]{1,0:T(8,128)(2,1)}, bf16[128,512]{1,0:T(8,128)(2,1)S(1)}, u32[]{:S(2)}) copy-start(bf16[128,512]{1,0:T(8,128)(2,1)S(1)} %fusion.10) | copy-start | bytes 393220
  181.4 5.0 %collective-permute-start.17 = (bf16[128,512]{1,0:T(8,128)(2,1)S(1)}, bf16[128,512]{1,0:T(8,128)(2,1)S(1)}, u32[]{:S(2)}, u32[]{:S(2)}) collective-permute-start(bf16[128,512]{1,0:T(8,128)(2,1)S(1)} %fusion.10), channel_id=1, source_target_pairs={{0,4},{4,0},{8,12},{12,8},{16,20},{20,16},{24,28},{28,24},{1,5},{5... | collective-permute-start | bytes 393224 | tf_op jit(solution)/shard_map/ppermute | solution.py:8
  186.5 6.4 %collective-permute-start.18 = (bf16[256,512]{1,0:T(8,128)(2,1)S(1)}, bf16[256,512]{1,0:T(8,128)(2,1)S(1)}, u32[]{:S(2)}, u32[]{:S(2)}) collective-permute-start(bf16[256,512]{1,0:T(8,128)(2,1)S(1)} %maximum_select_fusion.18), channel_id=1, source_target_pairs={{0,8},{4,12},{8,0},{12,4},{16,24},{20,28},{24,16},{28,20},{1,9},{5... | collective-permute-start | bytes 786440 | tf_op jit(solution)/shard_map/ppermute | solution.py:8
  195.9 6.4 %collective-permute-start.19 = (bf16[256,512]{1,0:T(8,128)(2,1)S(1)}, bf16[256,512]{1,0:T(8,128)(2,1)S(1)}, u32[]{:S(2)}, u32[]{:S(2)}) collective-permute-start(bf16[256,512]{1,0:T(8,128)(2,1)S(1)} %fusion.6), channel_id=1, source_target_pairs={{0,4},{4,0},{8,12},{12,8},{16,20},{20,16},{24,28},{28,24},{1,5},{5... | collective-permute-start | bytes 786440 | tf_op jit(solution)/shard_map/ppermute | solution.py:8
  202.7 12.8 %copy-start.5 = (bf16[256,512]{1,0:T(8,128)(2,1)}, bf16[256,512]{1,0:T(8,128)(2,1)S(1)}, u32[]{:S(2)}) copy-start(bf16[256,512]{1,0:T(8,128)(2,1)S(1)} %fusion.7) | copy-start | bytes 786436
  202.7 6.4 %collective-permute-start.20 = (bf16[256,512]{1,0:T(8,128)(2,1)S(1)}, bf16[256,512]{1,0:T(8,128)(2,1)S(1)}, u32[]{:S(2)}, u32[]{:S(2)}) collective-permute-start(bf16[256,512]{1,0:T(8,128)(2,1)S(1)} %fusion.7), channel_id=1, source_target_pairs={{0,4},{4,0},{8,12},{12,8},{16,20},{20,16},{24,28},{28,24},{1,5},{5... | collective-permute-start | bytes 786440 | tf_op jit(solution)/shard_map/ppermute | solution.py:8
  215.4 1.0 copy-start.21
  223.0 1.6 copy-start.2
  223.0 14.6 %copy-start.14 = (s32[8,2]{0,1:T(2,128)S(1)}, s32[8,2]{0,1:T(2,128)}, u32[]{:S(2)}) copy-start(s32[8,2]{0,1:T(2,128)} %param.31) | copy-start | bytes 196
  224.7 50.6 %collective-permute-start.24 = (bf16[2,1024,512]{1,2,0:T(8,128)(2,1)S(1)}, bf16[2,1024,512]{1,2,0:T(8,128)(2,1)}, u32[]{:S(2)}, u32[]{:S(2)}) collective-permute-start(bf16[2,1024,512]{1,2,0:T(8,128)(2,1)S(1)} %slice.90), channel_id=1, source_target_pairs={{8,0},{12,4},{16,8},{20,12},{24,16},{28,20},{9,1},{13,5},{17,9},{2... | collective-permute-start | bytes 6291464 | tf_op jit(solution)/shard_map/ppermute | solution.py:14
  225.9 51.8 %collective-permute-start.23 = (bf16[2,1024,512]{1,2,0:T(8,128)(2,1)S(1)}, bf16[2,1024,512]{1,2,0:T(8,128)(2,1)}, u32[]{:S(2)}, u32[]{:S(2)}) collective-permute-start(bf16[2,1024,512]{1,2,0:T(8,128)(2,1)S(1)} %slice.90), channel_id=1, source_target_pairs={{4,0},{8,4},{12,8},{16,12},{20,16},{24,20},{28,24},{5,1},{9,5},{13... | collective-permute-start | bytes 6291464 | tf_op jit(solution)/shard_map/ppermute | solution.py:14
  227.2 75.6 %collective-permute-start.22 = (bf16[2,1024,512]{1,2,0:T(8,128)(2,1)S(1)}, bf16[2,1024,512]{1,2,0:T(8,128)(2,1)}, u32[]{:S(2)}, u32[]{:S(2)}) collective-permute-start(bf16[2,1024,512]{1,2,0:T(8,128)(2,1)S(1)} %slice.90), channel_id=1, source_target_pairs={{0,4},{4,8},{8,12},{12,16},{16,20},{20,24},{24,28},{1,5},{5,9},{9,... | collective-permute-start | bytes 6291464 | tf_op jit(solution)/shard_map/ppermute | solution.py:14
  233.2 72.2 %collective-permute-start.21 = (bf16[2,1024,512]{1,2,0:T(8,128)(2,1)S(1)}, bf16[2,1024,512]{1,2,0:T(8,128)(2,1)}, u32[]{:S(2)}, u32[]{:S(2)}) collective-permute-start(bf16[2,1024,512]{1,2,0:T(8,128)(2,1)S(1)} %slice.90), channel_id=1, source_target_pairs={{0,8},{4,12},{8,16},{12,20},{16,24},{20,28},{1,9},{5,13},{9,17},{1... | collective-permute-start | bytes 6291464 | tf_op jit(solution)/shard_map/ppermute | solution.py:14
Sparse Core Ops, SparseCore 0:
  9.6 25.2 all-gather.1
where the time goes:
time: 322 us; the launch traced here: 319 us
  waiting for transfers between devices  191 us (59%)
  starting transfers between devices  50.7 us (16%)
  other arithmetic  30.4 us (9%)
  matrix products  17.6 us (5%)
  between operations  14.6 us (5%)
  local copies, waits for them, and re-layouts  14.5 us (5%)
    ppermute x21, waiting for transfers between devices, from_partner(): lax.ppermute(x, axis, [(i, i ^ 1 << bit) for i in range(lax.axis_size(axi...  107 us
    ppermute x4, waiting for transfers between devices, from_behind(): lax.ppermute(value, axis, [(source, source + steps) for source in range(l...  59.8 us
    ppermute x21, starting transfers between devices, from_partner(): lax.ppermute(x, axis, [(i, i ^ 1 << bit) for i in range(lax.axis_size(axi...  37.7 us
    all_gather x1, waiting for transfers between devices, local(): factor = lax.all_gather(leaf_inverse, 'col', axis=0, tiled=True)  23.4 us
    ppermute x4, starting transfers between devices, from_behind(): lax.ppermute(value, axis, [(source, source + steps) for source in range(l...  13 us
    reduce_sum x4, other arithmetic, local(): jnp.sum(jnp.where(matches, arrived.astype(jnp.float32), 0.0), axis=0)  10.3 us
    dot_general x1, matrix products, local(): jnp.einsum('stf,fp->stp', surface_coupling, volume, preferred_element_typ...  6.6 us
  transfers between devices with their start and end apart: 26, of which 24 were waited for; matrix products, arithmetic and copies ran while one was open for 4% of the time, Pallas kernels for 0%

commit v1 on v0

v1 whole, which is shorter than its diff:
```python
import jax
import jax.numpy as jnp
from jax import lax
from jax.sharding import PartitionSpec as P

BF = jnp.bfloat16
F32 = jnp.float32


def swap(x, bit):
    n = lax.axis_size("front")
    return lax.ppermute(x, "front", [(i, i ^ (1 << bit)) for i in range(n)])


def shifted(x, step):
    n = lax.axis_size("front")
    return lax.ppermute(
        x, "front", [(i, i + step) for i in range(max(0, -step), min(n, n - step))]
    )


def family(x, bits, axis):
    n = lax.axis_size("front")
    size = 1 << bits
    groups = [list(range(g, g + size)) for g in range(0, n, size)]
    return lax.all_gather(x, "front", axis=axis, tiled=True, axis_index_groups=groups)


def mm(a, b):
    return jnp.dot(a, b, preferred_element_type=F32)


def tmm(a, b):
    return lax.dot_general(a, b, (((0,), (0,)), ((), ())), preferred_element_type=F32)


def columns(x, bit):
    half = x.shape[1] // 2
    upper = (lax.axis_index("front") >> bit) & 1 == 1
    low, high = x[:, :half], x[:, half:]
    return jnp.where(upper, high, low), jnp.where(upper, low, high)


def rejoin(mine, other, bit):
    upper = (lax.axis_index("front") >> bit) & 1 == 1
    return jnp.where(
        upper,
        jnp.concatenate([other, mine], axis=1),
        jnp.concatenate([mine, other], axis=1),
    )


def local(
    leaf_load, leaf_inverse, leaf_coupling, leaf_rowmap,
    load_first, load_second, load_third,
    inverse_first, inverse_second, inverse_third,
    coupling_first, coupling_second, rowmap_first, rowmap_second,
    surface_coupling, neighbor_tiles,
):
    me = lax.axis_index("front")
    n = lax.axis_size("front")
    factor = lax.all_gather(leaf_inverse, "col", axis=0, tiled=True)
    inv1 = family(inverse_first, 1, 0)
    inv2 = family(inverse_second, 2, 0)
    inv3 = family(inverse_third, 3, 0)
    d_mat = family(coupling_first, 1, 1)
    e_mat = family(coupling_second, 2, 1)
    row1 = lax.dynamic_index_in_dim(rowmap_first, me >> 1, 0, keepdims=False)
    row2 = lax.dynamic_index_in_dim(rowmap_second, me >> 2, 0, keepdims=False)
    c_mat = leaf_coupling[leaf_rowmap[0]]
    d_mat = d_mat[row1]
    e_mat = e_mat[row2]
    load1 = family(load_first, 1, 0)
    load2 = family(load_second, 2, 0)
    load3 = family(load_third, 3, 0)

    start = mm(factor, leaf_load).astype(BF)
    part = mm(c_mat, start).astype(BF)
    keep, give = columns(part, 0)
    l1, _ = columns(load1, 0)
    rhs1 = (l1.astype(F32) - keep.astype(F32) - swap(give, 0).astype(F32)).astype(BF)
    y1 = mm(inv1, rhs1).astype(BF)
    part = mm(d_mat, y1).astype(BF)
    keep, give = columns(part, 1)
    l2, _ = columns(columns(load2, 0)[0], 1)
    rhs2 = (l2.astype(F32) - keep.astype(F32) - swap(give, 1).astype(F32)).astype(BF)
    y2 = mm(inv2, rhs2).astype(BF)
    part = mm(e_mat, y2).astype(BF)
    l3, _ = columns(columns(load3, 0)[0], 1)
    rhs3 = (l3.astype(F32) - part.astype(F32) - swap(part, 2).astype(F32)).astype(BF)
    s3 = mm(inv3, rhs3).astype(BF)
    pull2 = tmm(e_mat, s3).astype(BF)
    s2 = (y2.astype(F32) - mm(inv2, pull2)).astype(BF)
    both = jnp.concatenate([s2, s3], axis=0)
    both = rejoin(both, swap(both, 1), 1)
    sep = s2.shape[0]
    pull1 = tmm(d_mat, both[:sep]).astype(BF)
    s1 = (y1.astype(F32) - mm(inv1, pull1)).astype(BF)
    full = jnp.concatenate([s1, both], axis=0)
    full = rejoin(full, swap(full, 0), 0)
    s1 = full[:sep]
    pulled = tmm(c_mat, s1).astype(BF)
    volume = (start.astype(F32) - mm(factor, pulled)).astype(BF)

    def rows_of(x, bits, like):
        r = like.shape[0]
        return lax.dynamic_slice_in_dim(x, (me % (1 << bits)) * r, r, 0)

    out1 = rows_of(s1, 1, load_first)
    out2 = rows_of(full[sep : 2 * sep], 2, load_second)
    out3 = rows_of(full[2 * sep :], 3, load_third)

    own = lax.dynamic_index_in_dim(neighbor_tiles, me, 0, keepdims=False)
    first = mm(surface_coupling[1], volume).astype(BF)
    second = mm(surface_coupling[2], volume).astype(BF)
    zero = jnp.zeros_like(first)
    arrived = []
    for step in (-1, 1, -2, 2):
        dest = me + step
        block = jnp.where(own[0] == dest, first, jnp.where(own[1] == dest, second, zero))
        arrived.append(shifted(block, step))
    total = mm(surface_coupling[0], volume).astype(BF).astype(F32)
    for block in arrived:
        total = total + block.astype(F32)
    return volume, total.astype(BF), out1, out2, out3


def solution(mesh):
    return jax.shard_map(
        local,
        mesh=mesh,
        in_specs=(
            P("front", "col"), P(("front", "col"), None), P("front", None), P("front", None),
            P("front", "col"), P("front", "col"), P("front", "col"),
            P("front", None), P("front", None), P("front", None),
            P(None, "front"), P(None, "front"), P(), P(),
            P("front", None, None), P(),
        ),
        out_specs=(P("front", "col"),) * 5,
        check_vma=False,
    )
```

time: 322 us -> 255 us (0.79)
  waiting for transfers between devices: 191 us -> 38.5 us
  blocking collectives: 0 us -> 131 us
  starting transfers between devices: 50.7 us -> 18.2 us
  other arithmetic: 30.4 us -> 4.28 us
  matrix products: 17.6 us -> 27.8 us
  between operations: 14.6 us -> 19.6 us
    all_gather x0 -> x8, blocking collectives: none -> 131 us  [family(): lax.all_gather(x, 'front', axis=axis, tiled=True, axis_index_groups=groups)]
    ppermute x25 -> x9, waiting for transfers between devices: 167 us -> 37.8 us  [the longest x5 26.5 us: swap(): return lax.ppermute(x, 'front', [(i, i ^ 1 << bit) for i in range(n)])]
    ppermute x25 -> x9, starting transfers between devices: 50.7 us -> 18.2 us  [the longest x4 14.7 us: shifted(): lax.ppermute(x, 'front', [(i, i + step) for i in range(max(0, -step), min...]
    all_gather x1, waiting for transfers between devices: 23.4 us -> 0.02 us  [local(): factor = lax.all_gather(leaf_inverse, 'col', axis=0, tiled=True)]
    reduce_sum x4 -> x0, other arithmetic: 10.3 us -> none  [local(): jnp.sum(jnp.where(matches, arrived.astype(jnp.float32), 0.0), axis=0)]
    dot_general x13, matrix products: 17.6 us -> 27.8 us  [mm(): return jnp.dot(a, b, preferred_element_type=F32)]
    scatter x3 -> x0, other arithmetic: 8.05 us -> none  [the longest x2 5.43 us: local(): jnp.zeros((sep_order, panel_cols), jnp.bfloat16).at[row_map]]
    sub x3 -> x0, other arithmetic: 4.31 us -> none  [local(): embedded - partial_value]
  transfers between devices with their start and end apart: 26 -> 10, of which waited for: 24 -> 5; matrix products, arithmetic and copies ran while one was open for 4% -> 5% of each run, Pallas kernels for 0% -> 0%
where the time goes in v1:
time: 255 us; the launch traced here: 253 us
  blocking collectives  131 us (51%)
  waiting for transfers between devices  38.5 us (15%)
  matrix products  27.8 us (11%)
  between operations  19.6 us (8%)
  starting transfers between devices  18.2 us (7%)
  local copies, waits for them, and re-layouts  13.8 us (5%)
  other arithmetic  4.28 us (2%)
    all_gather x8, blocking collectives, family(): lax.all_gather(x, 'front', axis=axis, tiled=True, axis_index_groups=groups)  131 us
    dot_general x13, matrix products, mm(): return jnp.dot(a, b, preferred_element_type=F32)  27.8 us
    ppermute x5, waiting for transfers between devices, swap(): return lax.ppermute(x, 'front', [(i, i ^ 1 << bit) for i in range(n)])  26.5 us
    ppermute x4, starting transfers between devices, shifted(): lax.ppermute(x, 'front', [(i, i + step) for i in range(max(0, -step), min...  14.7 us
    ppermute x4, waiting for transfers between devices, shifted(): lax.ppermute(x, 'front', [(i, i + step) for i in range(max(0, -step), min...  11.3 us
  transfers between devices with their start and end apart: 10, of which 5 were waited for; matrix products, arithmetic and copies ran while one was open for 5% of the time, Pallas kernels for 0%

profile of v1, /device:TPU:0, one launch (start us, length us, event | category | flops | bytes accessed | tf_op | source)
XLA Modules:
  0.0 253.5 jit_solution(17102955924721506170)
XLA Ops:
  7.2 0.0 copy-start
  7.2 0.0 all-gather.2.cloned.1.call-start
  7.2 0.7 all-gather.2.cloned.1.call-update
  7.9 0.7 compare_select_fusion.2
  8.6 0.0 copy-start.13
  8.6 0.0 copy-start.3
  8.7 2.8 %gather_fusion = bf16[512,1024]{1,0:T(8,128)(2,1)} fusion(bf16[512,1024]{1,0:T(8,128)(2,1)S(1)} %copy-done, s32[1024]{0:T(1024)S(1)} %pad_clamp_fusion.2), kind=kCustom, calls=%fused_computation | custom fusion | bytes 2099200 | tf_op jit(solution)/shard_map/gather | solution.py:70
  11.5 0.8 compare_select_fusion
  12.3 9.9 %all_gather.30 = bf16[512,512]{1,0:T(8,128)(2,1)S(1)} all-gather(bf16[512,256]{1,0:T(8,128)(2,1)S(1)} %copy-done.3), channel_id=1, replica_groups={{0,4},{8,12},{16,20},{24,28},{1,5},{9,13},{17,21},{25,29},{2,6},{10,14}..., dimensions={1}, use_global_device_ids=true | all-gather | bytes 786432 | tf_op jit(solution)/shard_map/all_gather | solution.py:26
  22.2 8.3 %all_gather.29 = bf16[512,512]{1,0:T(8,128)(2,1)} all-gather(bf16[256,512]{1,0:T(8,128)(2,1)S(1)} %copy-done.4), channel_id=1, replica_groups={{0,4},{8,12},{16,20},{24,28},{1,5},{9,13},{17,21},{25,29},{2,6},{10,14}..., dimensions={0}, use_global_device_ids=true | all-gather | bytes 786432 | tf_op jit(solution)/shard_map/all_gather | solution.py:26
  30.4 7.3 %all_gather.28 = bf16[512,512]{1,0:T(8,128)(2,1)} all-gather(bf16[256,512]{1,0:T(8,128)(2,1)S(1)} %copy-done.5), channel_id=1, replica_groups={{0,4},{8,12},{16,20},{24,28},{1,5},{9,13},{17,21},{25,29},{2,6},{10,14}..., dimensions={0}, use_global_device_ids=true | all-gather | bytes 786432 | tf_op jit(solution)/shard_map/all_gather | solution.py:26
  37.8 14.8 %all_gather.31 = bf16[512,512]{1,0:T(8,128)(2,1)S(1)} all-gather(bf16[128,512]{1,0:T(8,128)(2,1)S(1)} %copy-done.7), channel_id=1, replica_groups={{0,4,8,12},{16,20,24,28},{1,5,9,13},{17,21,25,29},{2,6,10,14},{18,22,26..., dimensions={0}, use_global_device_ids=true | all-gather | bytes 655360 | tf_op jit(solution)/shard_map/all_gather | solution.py:26
  52.6 12.8 %all_gather.33 = bf16[512,512]{1,0:T(8,128)(2,1)S(1)} all-gather(bf16[512,128]{1,0:T(8,128)(2,1)S(1)} %copy-done.8), channel_id=1, replica_groups={{0,4,8,12},{16,20,24,28},{1,5,9,13},{17,21,25,29},{2,6,10,14},{18,22,26..., dimensions={1}, use_global_device_ids=true | all-gather | bytes 655360 | tf_op jit(solution)/shard_map/all_gather | solution.py:26
  65.4 31.6 %all_gather.34 = bf16[512,512]{1,0:T(8,128)(2,1)S(1)} all-gather(bf16[64,512]{1,0:T(8,128)(2,1)S(1)} %copy-done.10), channel_id=1, replica_groups={{0,4,8,12,16,20,24,28},{1,5,9,13,17,21,25,29},{2,6,10,14,18,22,26,30},{..., dimensions={0}, use_global_device_ids=true | all-gather | bytes 589824 | tf_op jit(solution)/shard_map/all_gather | solution.py:26
  97.0 0.0 all-gather.2.cloned.1.call-done
  97.1 3.2 %convolution_convert_fusion = bf16[1024,512]{1,0:T(8,128)(2,1)S(1)} fusion(bf16[1024,1024]{1,0:T(8,128)(2,1)} %all-gather.2.cloned.1.call-done, bf16[1024,512]{1,0:T(8,128)(2,1)} %param.16), kind=kOutput, calls=%fused_computation.23 | convolution fusion | flops 1074266112 | bytes 4194304 | tf_op jit(solution)/shard_map/dot_general | solution.py:30
  100.3 0.0 copy-start.15
  100.3 0.7 convolution_convert_fusion.2
  101.0 0.0 copy-start.2
  101.0 0.8 copy-done.2
  101.8 0.7 broadcast_select_fusion
  102.5 1.4 collective-permute-start
  104.0 2.0 gather_fusion.1
  105.9 2.0 gather_fusion.2
  107.9 0.0 copy-start.9
  108.0 2.7 %collective-permute-done = bf16[512,256]{1,0:T(8,128)(2,1)} collective-permute-done((bf16[512,256]{1,0:T(8,128)(2,1)}, bf16[512,256]{1,0:T(8,128)(2,1)}, u32[]{:S(2)}, u32[]{:S(2)}) %collective-permute-start) | collective-permute-done | bytes 262176 | tf_op jit(solution)/shard_map/ppermute | solution.py:12
  110.6 1.8 convolution_convert_fusion.5
  112.5 0.0 copy-start.6
  112.5 0.3 convolution_convert_fusion.4
  112.8 0.1 collective-permute-start.1
  112.9 14.7 %all_gather.32 = bf16[512,512]{1,0:T(8,128)(2,1)S(1)} all-gather(bf16[128,512]{1,0:T(8,128)(2,1)S(1)} %copy-done.9), channel_id=1, replica_groups={{0,4,8,12},{16,20,24,28},{1,5,9,13},{17,21,25,29},{2,6,10,14},{18,22,26..., dimensions={0}, use_global_device_ids=true | all-gather | bytes 655360 | tf_op jit(solution)/shard_map/all_gather | solution.py:26
  127.6 0.3 convolution_convert_fusion.9
  128.0 0.3 convolution_convert_fusion.8
  128.3 1.9 collective-permute-start.2
  130.1 31.8 %all_gather.35 = bf16[512,512]{1,0:T(8,128)(2,1)S(1)} all-gather(bf16[64,512]{1,0:T(8,128)(2,1)S(1)} %copy-done.11), channel_id=1, replica_groups={{0,4,8,12,16,20,24,28},{1,5,9,13,17,21,25,29},{2,6,10,14,18,22,26,30},{..., dimensions={0}, use_global_device_ids=true | all-gather | bytes 589824 | tf_op jit(solution)/shard_map/all_gather | solution.py:26
  161.9 0.3 convolution_convert_fusion.7
  162.2 0.8 fusion.26
  163.0 0.1 collective-permute-start.3
  163.1 6.4 %collective-permute-done.3 = bf16[1024,128]{0,1:T(8,128)(2,1)S(1)} collective-permute-done((bf16[1024,128]{0,1:T(8,128)(2,1)S(1)}, bf16[1024,128]{0,1:T(8,128)(2,1)S(1)}, u32[]{:S(2)}, u32[]{:S(2)}) %collective-permute-start.3) | collective-permute-done | bytes 262176 | tf_op jit(solution)/shard_map/ppermute | solution.py:12
  169.5 0.1 maximum_select_fusion.1
  169.6 1.9 fusion.24
  171.5 0.1 pad_maximum_fusion
  171.6 0.1 collective-permute-start.4
  171.7 0.1 constant_dynamic-slice_fusion.3
  171.7 0.5 fusion.46
  177.4 17.5 %collective-permute-done.4 = bf16[1536,256]{0,1:T(8,128)(2,1)} collective-permute-done((bf16[1536,256]{0,1:T(8,128)(2,1)S(1)}, bf16[1536,256]{0,1:T(8,128)(2,1)}, u32[]{:S(2)}, u32[]{:S(2)}) %collective-permute-start.4) | collective-permute-done | bytes 786464 | tf_op jit(solution)/shard_map/ppermute | solution.py:12
  194.9 1.8 maximum_select_fusion
  196.7 5.0 %fusion.10 = bf16[1024,512]{1,0:T(8,128)(2,1)} fusion(bf16[1024,512]{1,0:T(8,128)(2,1)} %copy-done.15, bf16[1024,1024]{1,0:T(8,128)(2,1)} %all-gather.2.cloned.1.call-done, bf16[512,1024]{1,0:T(8,128)(2,1)} %gather_fusion, bf16[1536,512]{0,1:T(8,128)(2,1)S(1)} %maximum_select_fusion), kind=kOutput, calls=%fused_computation.15 | convolution fusion | flops 1612709888 | bytes 5767168 | tf_op jit(solution)/shard_map/dot_general | solution.py:30
  201.7 3.3 %fusion.17 = bf16[512,1024]{1,0:T(8,128)(2,1)S(1)} fusion(bf16[1024,512]{1,0:T(8,128)(2,1)} %fusion.10, bf16[3,1024,1024]{2,1,0:T(8,128)(2,1)} %param.30), kind=kOutput, calls=%fused_computation.21 | convolution fusion | flops 1074266112 | bytes 4194304 | tf_op jit(solution)/shard_map/dot_general | solution.py:30
  205.0 5.1 %select_bitcast_fusion.3 = (bf16[1024,512]{0,1:T(8,128)(2,1)}, bf16[1024,512]{0,1:T(8,128)(2,1)}, bf16[1024,512]{0,1:T(8,128)(2,1)}, bf16[1024,512]{0,1:T(8,128)(2,1)}) fusion(bf16[512,1024]{1,0:T(8,128)(2,1)S(1)} %fusion.17, pred[]{:T(512)S(6)} %eq.44, pred[]{:T(512)S(6)} %eq.43, pred[]{:T(512)S(6)} %eq.50, pred[]{:T(512)S(6)} %eq.49, pred[]{:T(512)S(6)} %eq.48, ...), kind=kOutput, calls=%fused_computation.42 | convolution fusion | flops 1078460416 | bytes 8388616 | tf_op jit(solution)/shard_map/dot_general | solution.py:30
  210.1 1.3 collective-permute-start.5
  211.4 6.1 %collective-permute-start.6 = (bf16[1024,512]{0,1:T(8,128)(2,1)}, bf16[1024,512]{0,1:T(8,128)(2,1)}, u32[]{:S(2)}, u32[]{:S(2)}) collective-permute-start(bf16[1024,512]{0,1:T(8,128)(2,1)} %get-tuple-element.18), channel_id=1, source_target_pairs={{0,4},{4,8},{8,12},{12,16},{16,20},{20,24},{24,28},{1,5},{5,9},{9,... | collective-permute-start | bytes 3145736 | tf_op jit(solution)/shard_map/ppermute | solution.py:17
  217.5 1.3 collective-permute-start.7
  218.8 6.0 %collective-permute-start.8 = (bf16[1024,512]{0,1:T(8,128)(2,1)}, bf16[1024,512]{0,1:T(8,128)(2,1)}, u32[]{:S(2)}, u32[]{:S(2)}) collective-permute-start(bf16[1024,512]{0,1:T(8,128)(2,1)} %get-tuple-element.16), channel_id=1, source_target_pairs={{0,8},{4,12},{8,16},{12,20},{16,24},{20,28},{1,9},{5,13},{9,17},{1... | collective-permute-start | bytes 3145736 | tf_op jit(solution)/shard_map/ppermute | solution.py:17
  224.9 0.9 fusion.45
  225.8 0.8 copy.28
  226.7 0.9 constant_dynamic-slice_fusion.1
  227.6 0.8 copy.29
  228.3 0.1 constant_dynamic-slice_fusion
  228.5 0.7 copy.30
  229.2 10.2 %collective-permute-done.6 = bf16[1024,512]{0,1:T(8,128)(2,1)} collective-permute-done((bf16[1024,512]{0,1:T(8,128)(2,1)}, bf16[1024,512]{0,1:T(8,128)(2,1)}, u32[]{:S(2)}, u32[]{:S(2)}) %collective-permute-start.6) | collective-permute-done | bytes 1048608 | tf_op jit(solution)/shard_map/ppermute | solution.py:17
  239.4 1.1 collective-permute-done.7
  240.5 4.8 %fusion.7 = bf16[1024,512]{0,1:T(8,128)(2,1)S(1)} fusion(bf16[1024,512]{0,1:T(8,128)(2,1)} %collective-permute-done.8, bf16[1024,512]{0,1:T(8,128)(2,1)} %collective-permute-done.7, bf16[1024,512]{0,1:T(8,128)(2,1)} %collective-permute-done.6, bf16[1024,512]{0,1:T(8,128)(2,1)} %collective-permute-done.5, bf16[1024,512]{1,0:T(8,128)(2,1)} %fusion.10, ...), kind=kOutput, calls=%fused_computation.11 | convolution fusion | flops 1079508992 | bytes 8388608 | tf_op jit(solution)/shard_map/dot_general | solution.py:30
  245.3 1.3 copy.27
  (36 shorter events, 0.2 us)
Async XLA Ops:
  7.2 1.5 copy-start
  7.2 89.9 %all-gather.2.cloned.1.call-start = ((), (), s32[]{:S(2)}) async-start(), calls=%async_computation | async-start | bytes 2621440 | tf_op jit(solution)/shard_map/all_gather | solution.py:62
  8.6 2.8 %copy-start.13 = (s32[2,512]{1,0:T(2,128)S(1)}, s32[2,512]{1,0:T(2,128)}, u32[]{:S(2)}) copy-start(s32[2,512]{1,0:T(2,128)} %param.29) | copy-start | bytes 12292
  8.6 3.6 %copy-start.3 = (bf16[512,256]{1,0:T(8,128)(2,1)S(1)}, bf16[512,256]{1,0:T(8,128)(2,1)}, u32[]{:S(2)}) copy-start(bf16[512,256]{1,0:T(8,128)(2,1)} %param.26) | copy-start | bytes 786436
  8.7 13.5 %copy-start.4 = (bf16[256,512]{1,0:T(8,128)(2,1)S(1)}, bf16[256,512]{1,0:T(8,128)(2,1)}, u32[]{:S(2)}) copy-start(bf16[256,512]{1,0:T(8,128)(2,1)} %param.23) | copy-start | bytes 786436
  8.7 21.8 %copy-start.5 = (bf16[256,512]{1,0:T(8,128)(2,1)S(1)}, bf16[256,512]{1,0:T(8,128)(2,1)}, u32[]{:S(2)}) copy-start(bf16[256,512]{1,0:T(8,128)(2,1)} %param.20) | copy-start | bytes 786436
  11.4 26.3 %copy-start.7 = (bf16[128,512]{1,0:T(8,128)(2,1)S(1)}, bf16[128,512]{1,0:T(8,128)(2,1)}, u32[]{:S(2)}) copy-start(bf16[128,512]{1,0:T(8,128)(2,1)} %param.21) | copy-start | bytes 393220
  11.5 41.1 %copy-start.8 = (bf16[512,128]{1,0:T(8,128)(2,1)S(1)}, bf16[512,128]{1,0:T(8,128)(2,1)}, u32[]{:S(2)}) copy-start(bf16[512,128]{1,0:T(8,128)(2,1)} %param.27) | copy-start | bytes 393220
  11.5 54.0 %copy-start.10 = (bf16[64,512]{1,0:T(8,128)(2,1)S(1)}, bf16[64,512]{1,0:T(8,128)(2,1)}, u32[]{:S(2)}) copy-start(bf16[64,512]{1,0:T(8,128)(2,1)} %param.22) | copy-start | bytes 196612
  97.1 3.2 %copy-start.1 = (bf16[512,1024]{1,0:T(8,128)(2,1)S(1)}, bf16[512,1024]{1,0:T(8,128)(2,1)}, u32[]{:S(2)}) copy-start(bf16[512,1024]{1,0:T(8,128)(2,1)} %gather_fusion) | copy-start | bytes 3145732
  100.3 2.3 copy-start.15
  101.0 0.8 copy-start.2
  102.5 8.1 %collective-permute-start = (bf16[512,256]{1,0:T(8,128)(2,1)}, bf16[512,256]{1,0:T(8,128)(2,1)}, u32[]{:S(2)}, u32[]{:S(2)}) collective-permute-start(bf16[512,256]{1,0:T(8,128)(2,1)} %broadcast_select_fusion), channel_id=1, source_target_pairs={{0,4},{4,0},{8,12},{12,8},{16,20},{20,16},{24,28},{28,24},{1,5},{5... | collective-permute-start | bytes 786440 | tf_op jit(solution)/shard_map/ppermute | solution.py:12
  107.9 5.0 %copy-start.9 = (bf16[128,512]{1,0:T(8,128)(2,1)S(1)}, bf16[128,512]{1,0:T(8,128)(2,1)}, u32[]{:S(2)}) copy-start(bf16[128,512]{1,0:T(8,128)(2,1)} %param.24) | copy-start | bytes 393220
  112.5 49.4 %copy-start.6 = (bf16[256,512]{1,0:T(8,128)(2,1)}, bf16[256,512]{1,0:T(8,128)(2,1)S(1)}, u32[]{:S(2)}) copy-start(bf16[256,512]{1,0:T(8,128)(2,1)S(1)} %convolution_convert_fusion.5) | copy-start | bytes 786436
  112.5 17.6 %copy-start.11 = (bf16[64,512]{1,0:T(8,128)(2,1)S(1)}, bf16[64,512]{1,0:T(8,128)(2,1)}, u32[]{:S(2)}) copy-start(bf16[64,512]{1,0:T(8,128)(2,1)} %param.25) | copy-start | bytes 196612
  112.8 14.8 %collective-permute-start.1 = (bf16[512,128]{1,0:T(8,128)(2,1)S(1)}, bf16[512,128]{1,0:T(8,128)(2,1)S(1)}, u32[]{:S(2)}, u32[]{:S(2)}) collective-permute-start(bf16[512,128]{1,0:T(8,128)(2,1)S(1)} %broadcast_select_fusion.1), channel_id=1, source_target_pairs={{0,8},{4,12},{8,0},{12,4},{16,24},{20,28},{24,16},{28,20},{1,9},{5... | collective-permute-start | bytes 393224 | tf_op jit(solution)/shard_map/ppermute | solution.py:12
  128.3 33.6 %collective-permute-start.2 = (bf16[512,128]{1,0:T(8,128)(2,1)S(1)}, bf16[512,128]{1,0:T(8,128)(2,1)S(1)}, u32[]{:S(2)}, u32[]{:S(2)}) collective-permute-start(bf16[512,128]{1,0:T(8,128)(2,1)S(1)} %convolution_convert_fusion.8), channel_id=1, source_target_pairs={{0,16},{4,20},{8,24},{12,28},{16,0},{20,4},{24,8},{28,12},{1,17},{... | collective-permute-start | bytes 393224 | tf_op jit(solution)/shard_map/ppermute | solution.py:12
  163.0 8.6 %copy-start.12 = (s32[8,2]{0,1:T(2,128)S(1)}, s32[8,2]{0,1:T(2,128)}, u32[]{:S(2)}) copy-start(s32[8,2]{0,1:T(2,128)} %param.31) | copy-start | bytes 196
  163.0 6.4 %collective-permute-start.3 = (bf16[1024,128]{0,1:T(8,128)(2,1)S(1)}, bf16[1024,128]{0,1:T(8,128)(2,1)S(1)}, u32[]{:S(2)}, u32[]{:S(2)}) collective-permute-start(bf16[1024,128]{0,1:T(8,128)(2,1)S(1)} %pad_maximum_fusion.1), channel_id=1, source_target_pairs={{0,8},{4,12},{8,0},{12,4},{16,24},{20,28},{24,16},{28,20},{1,9},{5... | collective-permute-start | bytes 786440 | tf_op jit(solution)/shard_map/ppermute | solution.py:12
  171.6 23.3 %collective-permute-start.4 = (bf16[1536,256]{0,1:T(8,128)(2,1)S(1)}, bf16[1536,256]{0,1:T(8,128)(2,1)}, u32[]{:S(2)}, u32[]{:S(2)}) collective-permute-start(bf16[1536,256]{0,1:T(8,128)(2,1)S(1)} %pad_maximum_fusion), channel_id=1, source_target_pairs={{0,4},{4,0},{8,12},{12,8},{16,20},{20,16},{24,28},{28,24},{1,5},{5... | collective-permute-start | bytes 2359304 | tf_op jit(solution)/shard_map/ppermute | solution.py:12
  201.7 3.3 %copy-start.14 = (bf16[1024,512]{1,0:T(8,128)(2,1)S(1)}, bf16[1024,512]{1,0:T(8,128)(2,1)}, u32[]{:S(2)}) copy-start(bf16[1024,512]{1,0:T(8,128)(2,1)} %fusion.10) | copy-start | bytes 3145732
  210.1 19.0 %collective-permute-start.5 = (bf16[1024,512]{0,1:T(8,128)(2,1)}, bf16[1024,512]{0,1:T(8,128)(2,1)}, u32[]{:S(2)}, u32[]{:S(2)}) collective-permute-start(bf16[1024,512]{0,1:T(8,128)(2,1)} %get-tuple-element.15), channel_id=1, source_target_pairs={{4,0},{8,4},{12,8},{16,12},{20,16},{24,20},{28,24},{5,1},{9,5},{13... | collective-permute-start | bytes 3145736 | tf_op jit(solution)/shard_map/ppermute | solution.py:17
  211.4 28.0 %collective-permute-start.6 = (bf16[1024,512]{0,1:T(8,128)(2,1)}, bf16[1024,512]{0,1:T(8,128)(2,1)}, u32[]{:S(2)}, u32[]{:S(2)}) collective-permute-start(bf16[1024,512]{0,1:T(8,128)(2,1)} %get-tuple-element.18), channel_id=1, source_target_pairs={{0,4},{4,8},{8,12},{12,16},{16,20},{20,24},{24,28},{1,5},{5,9},{9,... | collective-permute-start | bytes 3145736 | tf_op jit(solution)/shard_map/ppermute | solution.py:17
  217.5 22.9 %collective-permute-start.7 = (bf16[1024,512]{0,1:T(8,128)(2,1)}, bf16[1024,512]{0,1:T(8,128)(2,1)}, u32[]{:S(2)}, u32[]{:S(2)}) collective-permute-start(bf16[1024,512]{0,1:T(8,128)(2,1)} %get-tuple-element.17), channel_id=1, source_target_pairs={{8,0},{12,4},{16,8},{20,12},{24,16},{28,20},{9,1},{13,5},{17,9},{2... | collective-permute-start | bytes 3145736 | tf_op jit(solution)/shard_map/ppermute | solution.py:17
  218.8 21.7 %collective-permute-start.8 = (bf16[1024,512]{0,1:T(8,128)(2,1)}, bf16[1024,512]{0,1:T(8,128)(2,1)}, u32[]{:S(2)}, u32[]{:S(2)}) collective-permute-start(bf16[1024,512]{0,1:T(8,128)(2,1)} %get-tuple-element.16), channel_id=1, source_target_pairs={{0,8},{4,12},{8,16},{12,20},{16,24},{20,28},{1,9},{5,13},{9,17},{1... | collective-permute-start | bytes 3145736 | tf_op jit(solution)/shard_map/ppermute | solution.py:17
Sparse Core Ops, SparseCore 0:
  9.6 25.2 all-gather.1
